TPU v7x, 32 devices: a whole 2x2x4 slice. The times are simulated.
32 devices in a mesh: row: 4 (over y, core), col: 8 (over z, x).
Axes of the slice: x: 2, y: 2, z: 4, core: 2. Of those that a mesh axis runs over, the one named last changes fastest.
Arguments:
- grad_out: bfloat16 [2048, 8192], P('col', 'row'), may hold values from -0.09375 to 0.09375
- activations: bfloat16 [2048, 28672], P('row', 'col'), may hold values from -6 to 6
- left_steps: float32 [10, 8192], P(None, 'row')
- left_curves: float32 [10, 8192], P(None, 'row'), as said below
- right_steps: float32 [10, 28672], P(None, 'col')
- right_curves: float32 [10, 28672], P(None, 'col'), as said below
Outputs:
- direction: float32 [8192, 28672], P('row', 'col')
Inputs may be any that keep to these rules, and one draw needn't show every extreme that they name: `left_curves`: each curve row is its step row scaled entrywise by positive factors, so every step has a positive inner product with its curve; the last pair is the newest. `right_curves`: as for the output side.
All inputs are finite; a program needn't handle non-finite values.
Results may differ from a plain program's by a relative error of at most 0.0003.
Values may be sent and summed in bfloat16 or wider, within the bound.
A program may use at most 192 MiB of HBM per device.

v0:
```python
import jax
import jax.numpy as jnp
from jax import lax
from jax.sharding import PartitionSpec as P

HIGH = lax.Precision.HIGHEST


def upper_inverse(upper_tri):
    count = upper_tri.shape[0]
    identity = jnp.eye(count, dtype=upper_tri.dtype)
    inv_rows = [None] * count
    for index in reversed(range(count)):
        running = identity[index]
        for later in range(index + 1, count):
            running = running - upper_tri[index, later] * inv_rows[later]
        inv_rows[index] = running / upper_tri[index, index]
    return jnp.stack(inv_rows, 0)


def compact(pair_sy, pair_yy):
    scaling = pair_sy[-1, -1] / pair_yy[-1, -1]
    upper_tri = jnp.triu(pair_sy)
    inverse = upper_inverse(upper_tri)
    middle = jnp.diag(jnp.diag(pair_sy)) + scaling * pair_yy
    return (scaling, inverse, middle)


def pair_products(step_rows, curv_rows):
    pair_sy = jnp.dot(step_rows, curv_rows.T, precision=HIGH, preferred_element_type=jnp.float32)
    pair_yy = jnp.dot(curv_rows, curv_rows.T, precision=HIGH, preferred_element_type=jnp.float32)
    return (pair_sy, pair_yy)


def apply_left(grad_block, step_rows, curv_rows, terms, proj_steps, proj_curves):
    scaling, inverse, middle = terms
    weighted = jnp.dot(inverse, proj_steps, precision=HIGH)
    coeffs = jnp.dot(
        inverse.T, jnp.dot(middle, weighted, precision=HIGH) - scaling * proj_curves, precision=HIGH
    )
    lefted = (
        scaling * grad_block
        + jnp.dot(step_rows.T, coeffs, precision=HIGH)
        - scaling * jnp.dot(curv_rows.T, weighted, precision=HIGH)
    )
    return (lefted, weighted, coeffs)


def apply_right(lefted, step_rows, curv_rows, terms, side_steps, side_curves):
    scaling, inverse, middle = terms
    weighted = jnp.dot(side_steps, inverse.T, precision=HIGH)
    coeffs = jnp.dot(
        jnp.dot(weighted, middle, precision=HIGH) - scaling * side_curves, inverse, precision=HIGH
    )
    return (
        scaling * lefted
        + jnp.dot(coeffs, step_rows, precision=HIGH)
        - scaling * jnp.dot(weighted, curv_rows, precision=HIGH)
    )


def on_device(grad_out, activations, left_steps, left_curves, right_steps, right_curves):
    contract = (((0,), (0,)), ((), ()))
    pairs = left_steps.shape[0]
    left_pair = jnp.concatenate([left_steps, left_curves], 0)
    right_pair = jnp.concatenate([right_steps, right_curves], 0)
    left_sy, left_yy = pair_products(left_steps, left_curves)
    right_sy, right_yy = pair_products(right_steps, right_curves)
    token_panel = lax.all_gather(activations, "row", axis=0, tiled=True)
    left_part = jnp.dot(grad_out.astype(jnp.float32), left_pair.T, precision=HIGH)
    right_part = jnp.dot(token_panel.astype(jnp.float32), right_pair.T, precision=HIGH)
    left_sy, left_yy, left_part = lax.psum((left_sy, left_yy, left_part), "row")
    right_sy, right_yy, right_part = lax.psum((right_sy, right_yy, right_part), "col")
    shard_piece = lax.all_gather(grad_out, "col", axis=0, tiled=True)
    block = lax.dot_general(shard_piece, token_panel, contract, preferred_element_type=jnp.float32)
    grad_right = lax.dot_general(
        shard_piece.astype(jnp.float32), right_part, contract, precision=HIGH
    )
    left_full = lax.all_gather(left_part, "col", axis=0, tiled=True)
    proj_both = lax.dot_general(
        left_full, token_panel.astype(jnp.float32), contract, precision=HIGH
    )
    left_terms = compact(left_sy, left_yy)
    lefted, weighted, coeffs = apply_left(
        block, left_steps, left_curves, left_terms, proj_both[:pairs], proj_both[pairs:]
    )
    coeff_fix, weight_fix = lax.psum(
        (
            jnp.dot(coeffs, right_pair.T, precision=HIGH),
            jnp.dot(weighted, right_pair.T, precision=HIGH),
        ),
        "col",
    )
    l_scale = left_terms[0]
    both_side = (
        l_scale * grad_right
        + jnp.dot(left_steps.T, coeff_fix, precision=HIGH)
        - l_scale * jnp.dot(left_curves.T, weight_fix, precision=HIGH)
    )
    side_steps, side_curves = (both_side[:, :pairs], both_side[:, pairs:])
    return apply_right(
        lefted, right_steps, right_curves, compact(right_sy, right_yy), side_steps, side_curves
    )


def solution(mesh):
    in_specs = (
        P("col", "row"),
        P("row", "col"),
        P(None, "row"),
        P(None, "row"),
        P(None, "col"),
        P(None, "col"),
    )
    out_specs = P("row", "col")
    return jax.shard_map(
        on_device, mesh=mesh, in_specs=in_specs, out_specs=out_specs, check_vma=False
    )
```

profile of v0, /device:TPU:0, one launch (start us, length us, event | category | flops | bytes accessed | tf_op | source)
XLA Modules:
  0.0 438.2 jit_solution(18301320806009229148)
XLA Ops:
  6.5 0.0 copy-start
  6.5 0.0 copy-start.1
  6.5 0.0 all-gather.5.cloned.1.call-start
  6.5 0.7 all-gather.5.cloned.1.call-update
  7.3 0.0 copy-start.2
  7.3 0.0 all-gather.3.cloned.1.call-start
  7.3 0.7 all-gather.3.cloned.1.call-update
  8.0 0.0 all-reduce.4.cloned.1.call-start
  8.1 1.2 fusion.44
  9.3 1.3 fusion.43
  10.6 2.4 convolution_bitcast_fusion.1
  12.9 13.3 %all-reduce.1 = (f32[10,10]{1,0:T(8,128)S(1)}, f32[256,20]{0,1:T(8,128)S(1)}, f32[10,10]{1,0:T(8,128)S(1)}) all-reduce(f32[10,10]{1,0:T(8,128)S(1)} %fusion.43, f32[256,20]{0,1:T(8,128)S(1)} %convolution_bitcast_fusion.1, f32[10,10]{1,0:T(8,128)S(1)} %fusion.44), channel_id=1, replica_groups=mesh['row'=4,'col'=8] {'row'}, use_global_device_ids=true, to_apply=%region_2.0 | all-reduce | flops 5320 | bytes 42560 | tf_op jit(solution)/shard_map/psum | solution.py:72
  26.2 0.6 slice.548
  26.8 0.7 slice.549
  27.5 0.7 gather_fusion
  29.6 0.1 fusion.21
  29.7 0.7 fusion.38
  30.4 0.7 fusion.39
  31.1 0.7 fusion.40
  31.8 34.3 %subtract_divide_fusion.9 = (f32[1,10]{1,0:T(1,128)S(1)}, f32[1,10]{1,0:T(1,128)S(1)}, f32[1,10]{1,0:T(1,128)S(1)}, f32[1,10]{1,0:T(1,128)S(1)}, f32[1,10]{1,0:T...) fusion(f32[10,10]{1,0:T(8,128)S(1)} %fusion.22, ...), kind=kLoop, calls=%fused_computation.55 | loop fusion | flops 1000 | bytes 1020 | tf_op jit(solution)/shard_map/div | solution.py:17
  66.2 31.0 %all_gather.11 = f32[2048,20]{0,1:T(8,128)S(1)} all-gather(f32[256,20]{0,1:T(8,128)S(1)} %get-tuple-element.10), channel_id=1, replica_groups=mesh['row'=4,'col'=8] {'col'}, dimensions={0}, use_global_device_ids=true | all-gather | bytes 184320 | tf_op jit(solution)/shard_map/all_gather | solution.py:79
  97.2 1.4 fusion.42
  98.7 1.5 fusion.41
  100.1 5.7 %all-gather.5.cloned.1.call-done = bf16[2048,3584]{1,0:T(8,128)(2,1)} async-done(((bf16[512,3584]{1,0:T(8,128)(2,1)}), bf16[2048,3584]{1,0:T(8,128)(2,1)}) %all-gather.5.cloned.1.call-update) | async-done | bytes 14680080 | tf_op jit(solution)/shard_map/all_gather | solution.py:69
  105.8 9.0 %fusion.45 = f32[20,3584]{1,0:T(8,128)S(1)} fusion(f32[2048,20]{0,1:T(8,128)S(1)} %all_gather.11, bf16[2048,3584]{1,0:T(8,128)(2,1)} %all-gather.5.cloned.1.call-done), kind=kOutput, calls=%fused_computation.83 | convolution fusion | flops 1761607680 | bytes 15130624 | tf_op jit(solution)/shard_map/dot_general | solution.py:80
  114.8 0.3 fusion.5
  115.1 0.0 copy-done
  115.2 0.0 copy-done.1
  115.2 0.5 fusion.12
  115.6 0.4 convolution_subtract_fusion
  116.0 0.4 fusion.46
  116.4 0.5 fusion.13
  116.9 38.7 %all-reduce = (f32[10,10]{1,0:T(8,128)S(1)}, f32[10,20]{1,0:T(8,128)S(1)}, f32[10,20]{1,0:T(8,128)S(1)}, f32[10,10]{1,0:T(8,128)S(1)}) all-reduce(f32[10,10]{1,0:T(8,128)S(1)} %fusion.41, f32[10,20]{1,0:T(8,128)S(1)} %fusion.12, f32[10,20]{1,0:T(8,128)S(1)} %fusion.13, f32[10,10]{1,0:T(8,128)S(1)} %fusion.42), channel_id=1, replica_groups=mesh['row'=4,'col'=8] {'col'}, use_global_device_ids=true, to_apply=%region_0.0 | all-reduce | flops 600 | bytes 4800 | tf_op jit(solution)/shard_map/psum | solution.py:73
  155.6 0.6 slice.546
  156.3 0.7 gather_fusion.1
  157.0 0.6 slice.547
  157.6 0.1 fusion.20
  157.7 0.7 fusion.35
  158.4 0.0 copy-start.3
  158.4 0.7 fusion.36
  159.1 0.7 fusion.37
  159.9 16.2 %convolution_bitcast_fusion = f32[2048,20]{0,1:T(8,128)} fusion(bf16[2048,3584]{1,0:T(8,128)(2,1)} %all-gather.5.cloned.1.call-done, f32[10,3584]{1,0:T(8,128)S(1)} %copy-done, f32[10,3584]{1,0:T(8,128)S(1)} %copy-done.1), kind=kOutput, calls=%fused_computation.10 | convolution fusion | flops 1761679360 | bytes 15130624 | tf_op jit(solution)/shard_map/dot_general | solution.py:71
  176.1 0.0 copy-done.2
  176.1 26.7 %fusion.48 = f32[3584,2048]{0,1:T(8,128)} fusion(f32[10,3584]{1,0:T(8,128)S(1)} %fusion.5, f32[10,2048]{1,0:T(8,128)S(1)} %copy-done.2), kind=kOutput, calls=%fused_computation.86 | convolution fusion | flops 880803840 | bytes 29585408 | tf_op jit(solution)/shard_map/dot_general | solution.py:44
  202.8 0.0 copy-done.3
  202.8 26.9 %fusion.47 = f32[3584,2048]{0,1:T(8,128)} fusion(f32[10,3584]{1,0:T(8,128)S(1)} %fusion.46, f32[10,2048]{1,0:T(8,128)S(1)} %copy-done.3), kind=kOutput, calls=%fused_computation.85 | convolution fusion | flops 880803840 | bytes 29585408 | tf_op jit(solution)/shard_map/dot_general | solution.py:43
  229.7 0.0 all-reduce.4.cloned.1.call-update
  231.1 34.3 %subtract_divide_fusion = (f32[1,10]{1,0:T(1,128)S(1)}, f32[1,10]{1,0:T(1,128)S(1)}, f32[1,10]{1,0:T(1,128)S(1)}, f32[1,10]{1,0:T(1,128)S(1)}, f32[1,10]{1,0:T(1...) fusion(f32[10,10]{1,0:T(8,128)S(1)} %fusion.22, ...), kind=kLoop, calls=%fused_computation.46 | loop fusion | flops 1000 | bytes 1020 | tf_op jit(solution)/shard_map/div | solution.py:17
  265.4 0.4 convolution_multiply_fusion
  265.8 0.0 all-gather.3.cloned.1.call-done
  265.8 39.8 %all-reduce.4.cloned.1.call-done = f32[2048,20]{0,1:T(8,128)} async-done(((f32[2048,20]{0,1:T(8,128)}), f32[2048,20]{0,1:T(8,128)}) %all-reduce.4.cloned.1.call-update) | async-done | bytes 163856 | tf_op jit(solution)/shard_map/psum | solution.py:73
  305.6 5.7 %convolution_multiply_fusion.1 = f32[20,2048]{1,0:T(8,128)S(1)} fusion(f32[2048,20]{0,1:T(8,128)} %all-reduce.4.cloned.1.call-done, bf16[2048,2048]{1,0:T(8,128)(2,1)} %all-gather.3.cloned.1.call-done, f32[]{:T(128)} %bitcast.1), kind=kOutput, calls=%fused_computation.13 | convolution fusion | flops 1006673920 | bytes 8716292 | tf_op jit(solution)/shard_map/dot_general | solution.py:76
  311.3 0.4 fusion.4
  311.7 0.3 fusion.10
  311.9 27.2 %fusion.51 = f32[2048,3584]{1,0:T(8,128)} fusion(f32[2048,10]{0,1:T(8,128)S(1)} %fusion.10, f32[10,3584]{1,0:T(8,128)S(1)} %copy-done), kind=kOutput, calls=%fused_computation.89 | convolution fusion | flops 880803840 | bytes 29585408 | tf_op jit(solution)/shard_map/dot_general | solution.py:58
  339.1 0.4 convolution_subtract_fusion.1
  339.5 1.8 fusion.49
  341.3 26.6 %fusion.50 = f32[2048,3584]{1,0:T(8,128)} fusion(f32[2048,10]{1,0:T(8,128)S(1)} %fusion.49, f32[10,3584]{1,0:T(8,128)S(1)} %copy-done.1), kind=kOutput, calls=%fused_computation.88 | convolution fusion | flops 880803840 | bytes 29585408 | tf_op jit(solution)/shard_map/dot_general | solution.py:57
  367.9 63.5 %fusion.2 = f32[2048,3584]{1,0:T(8,128)} fusion(f32[2048,3584]{1,0:T(8,128)} %fusion.50, f32[3584,2048]{0,1:T(8,128)} %fusion.47, f32[2048,3584]{1,0:T(8,128)} %fusion.51, f32[3584,2048]{0,1:T(8,128)} %fusion.48, bf16[2048,2048]{1,0:T(8,128)(2,1)} %all-gather.3.cloned.1.call-done, bf16[2048,3584]{1,0:T(8,128)(2,1)} %all-gather.5.cloned.1.call-done, ...), kind=kOutput, calls=%fused_computation.5 | convolution fusion | flops 30123491328 | bytes 169869312 | tf_op jit(solution)/shard_map/dot_general | solution.py:75
  (5 shorter events, 0.1 us)
Async XLA Ops:
  6.5 108.6 %copy-start = (f32[10,3584]{1,0:T(8,128)S(1)}, f32[10,3584]{1,0:T(8,128)}, u32[]{:S(2)}) copy-start(f32[10,3584]{1,0:T(8,128)} %param.11) | copy-start | bytes 430084
  6.5 108.6 %copy-start.1 = (f32[10,3584]{1,0:T(8,128)S(1)}, f32[10,3584]{1,0:T(8,128)}, u32[]{:S(2)}) copy-start(f32[10,3584]{1,0:T(8,128)} %param.10) | copy-start | bytes 430084
  6.5 99.2 %all-gather.5.cloned.1.call-start = ((), (), s32[]{:S(2)}) async-start(), calls=%async_computation.1 | async-start | bytes 18350080 | tf_op jit(solution)/shard_map/all_gather | solution.py:69
  7.3 168.8 %copy-start.2 = (f32[10,2048]{1,0:T(8,128)S(1)}, f32[10,2048]{1,0:T(8,128)}, u32[]{:S(2)}) copy-start(f32[10,2048]{1,0:T(8,128)} %param.9) | copy-start | bytes 245764
  7.3 258.5 %all-gather.3.cloned.1.call-start = ((), (), s32[]{:S(2)}) async-start(), calls=%async_computation | async-start | bytes 9437184 | tf_op jit(solution)/shard_map/all_gather | solution.py:74
  8.0 297.6 %all-reduce.4.cloned.1.call-start = ((), (), s32[]{:S(2)}) async-start(), calls=%async_computation.2 | async-start | bytes 393216 | tf_op jit(solution)/shard_map/psum | solution.py:73
  158.4 44.4 %copy-start.3 = (f32[10,2048]{1,0:T(8,128)S(1)}, f32[10,2048]{1,0:T(8,128)}, u32[]{:S(2)}) copy-start(f32[10,2048]{1,0:T(8,128)} %param.8) | copy-start | bytes 245764
Sparse Core Ops, SparseCore 0:
  8.9 96.8 all-gather.4
  107.9 126.0 all-gather.2
  237.3 68.2 all-reduce.3
where the time goes:
time: 445 us; the launch traced here: 438 us
  matrix products  215 us (48%)
  blocking collectives  83 us (19%)
  other arithmetic  68.8 us (15%)
  waiting for transfers between devices  46.9 us (11%)
  between operations  16.2 us (4%)
  local copies, waits for them, and re-layouts  8.38 us (2%)
    div x2, other arithmetic, upper_inverse(): inv_rows[index] = running / upper_tri[index, index]  68.6 us
    dot_general x1, matrix products, on_device(): lax.dot_general(shard_piece, token_panel, contract, preferred_element_typ...  63.5 us
    psum x1, waiting for transfers between devices, on_device(): lax.psum((right_sy, right_yy, right_part), 'col')  39.8 us
    psum x1, blocking collectives, on_device(): lax.psum((right_sy, right_yy, right_part), 'col')  38.7 us
    all_gather x1, blocking collectives, on_device(): left_full = lax.all_gather(left_part, 'col', axis=0, tiled=True)  31 us
    dot_general x1, matrix products, apply_right(): jnp.dot(weighted, curv_rows, precision=HIGH)  27.2 us
    dot_general x1, matrix products, apply_left(): jnp.dot(step_rows.T, coeffs, precision=HIGH)  26.9 us
    dot_general x1, matrix products, apply_left(): jnp.dot(curv_rows.T, weighted, precision=HIGH)  26.7 us
  transfers between devices with their start and end apart: 3, of which 2 were waited for; matrix products, arithmetic and copies ran while one was open for 38% of the time, Pallas kernels for 0%

commit v1 on v0

v1 whole, which is shorter than its diff:
```python
import functools
import jax
import jax.numpy as jnp
from jax import lax
from jax.experimental import pallas as pl
from jax.experimental.pallas import tpu as pltpu
from jax.sharding import PartitionSpec as P

HIGH = lax.Precision.HIGHEST
MESH = pl.DeviceIdType.MESH
F32, BF16 = jnp.float32, jnp.bfloat16
HALF = 16
BOTH = 2 * HALF


def dot(a, b, ca, cb):
    return lax.dot_general(a, b, (((ca,), (cb,)), ((), ())), precision=HIGH, preferred_element_type=F32)


def bdot(a, b, ca, cb):
    return lax.dot_general(a, b, (((ca,), (cb,)), ((), ())), preferred_element_type=F32)


def pieces(x, count):
    out = []
    for _ in range(count):
        top = x.astype(BF16).astype(F32)
        out.append(top)
        x = x - top
    return out


def times_pieces(x, mat):
    rows = x.shape[0]
    got = bdot(jnp.concatenate(pieces(x, 3), 0).astype(BF16), mat, 1, 1)
    return got[:rows] + got[rows : 2 * rows] + got[2 * rows :]


def compact(prod, pairs):
    sub = lax.broadcasted_iota(jnp.int32, (HALF, HALF), 0)
    lane = lax.broadcasted_iota(jnp.int32, (HALF, HALF), 1)
    sy, yy = prod[:HALF], prod[HALF:]

    def pick(x, mask, axes):
        x = jnp.where(mask, x, 0.0)
        for axis in axes:
            x = jnp.sum(x, axis=axis, keepdims=True)
        return x

    last = (sub == pairs - 1) & (lane == pairs - 1)
    scaling = pick(sy, last, (0, 1)) / pick(yy, last, (0, 1))
    upper = jnp.where(sub <= lane, sy, 0.0)
    inv = jnp.where((sub == lane) & (sub < pairs), 1.0, 0.0)
    for j in reversed(range(pairs)):
        column = pick(upper, lane == j, (1,))
        row = pick(inv, sub == j, (0,)) / pick(upper, (sub == j) & (lane == j), (0, 1))
        inv = jnp.where(sub == j, row, jnp.where(sub < j, inv - column * row, inv))
    middle = jnp.where(sub == lane, sy, 0.0) + scaling * yy
    return scaling, inv, middle


def apply_terms(terms, x):
    scaling, inv, middle = terms
    weighted = dot(inv, x[:HALF], 1, 0)
    coeffs = dot(inv, dot(middle, weighted, 1, 0) - scaling * x[HALF:], 0, 0)
    return jnp.concatenate([coeffs, -scaling * weighted], 0)


def stages(n):
    return n.bit_length() - 1


def gather_kernel(
    nrow, ncol, pairs, aligned, cuts, spread,
    act, go, lpair, rpair,
    act_full, gt_full, lf_out, rf_out, x2_out, s_out,
    gt, act_v, l_msg, r_msg, l_in, r_in, l_sum, r_sum, l_all, r_all, l_cat, r_cat,
    local_sem, cw_s, cw_r, cc_s, cc_r, y_s, y_r, sib_s, sib_r,
    l1_s, l1_r, r1_s, r1_r, l2_s, l2_r, r2_s, r2_r,
):
    r, c = lax.axis_index("row"), lax.axis_index("col")
    tok_r, tok_c, dloc = act.shape[0], go.shape[0], go.shape[1]
    ny = nrow // 2
    y, core = r // 2, r % 2
    nz = ncol // 2

    def dev(row, col):
        return {"row": row, "col": col}

    barrier = pltpu.get_barrier_semaphore()
    for d in range(1, nrow):
        pl.semaphore_signal(barrier, inc=1, device_id=dev((r + d) % nrow, c), device_id_type=MESH)
    for d in range(1, ncol):
        pl.semaphore_signal(barrier, inc=1, device_id=dev(r, (c + d) % ncol), device_id_type=MESH)
    pl.semaphore_wait(barrier, nrow + ncol - 2)

    pending = []

    def remote(src, dst, send, recv, row, col):
        copy = pltpu.make_async_remote_copy(
            src_ref=src, dst_ref=dst, send_sem=send, recv_sem=recv,
            device_id=dev(row, col), device_id_type=MESH)
        copy.start()
        pending.append(copy)
        return copy

    def local(src, dst, sem):
        copy = pltpu.make_async_copy(src, dst, sem)
        copy.start()
        return copy

    step_a = tok_r // (2 * cuts)

    def act_at(row, part):
        start = row * tok_r + part * step_a
        return act_full.at[pl.ds(pl.multiple_of(start, 16), step_a), :]

    def y_parts(k, way):
        full = ny // 2 - 1
        mine = range(way * cuts, (way + 1) * cuts)
        other = range((1 - way) * cuts, (2 - way) * cuts)
        return list(mine) + (list(other) if k < full else [])

    def y_send(k, way, part):
        sign = 1 - 2 * way
        origin = ((y - sign * k + ny) % ny) * 2 + core
        target = ((y + sign + ny) % ny) * 2 + core
        src = act.at[pl.ds(part * step_a, step_a), :] if k == 0 else act_at(origin, part)
        idx = (way, k, part)
        remote(src, act_at(origin, part), y_s.at[idx], y_r.at[idx], target, c)

    def y_wait(k, way, part):
        sign = 1 - 2 * way
        origin = ((y - sign * (k + 1) + 2 * ny) % ny) * 2 + core
        piece = act_at(origin, part)
        idx = (way, k, part)
        pltpu.make_async_remote_copy(
            src_ref=piece, dst_ref=piece, send_sem=y_s.at[idx], recv_sem=y_r.at[idx],
            device_id=dev(r, c), device_id_type=MESH).wait_recv()
        remote(piece, piece, sib_s.at[idx], sib_r.at[idx], y * 2 + 1 - core, c)
        if k + 1 < max(ny // 2, 1) and part in y_parts(k + 1, way):
            y_send(k + 1, way, part)

    for part in range(cuts):
        y_send(0, 0, part)
        y_send(0, 1, cuts + part)
    if ny > 2:
        for part in range(cuts):
            y_send(0, 0, cuts + part)
            y_send(0, 1, part)
    own_act = act_full.at[pl.ds(pl.multiple_of(r * tok_r, 16), tok_r), :]
    own_sib = pltpu.make_async_remote_copy(
        src_ref=act, dst_ref=own_act, send_sem=local_sem.at[3], recv_sem=local_sem.at[4],
        device_id=dev(y * 2 + 1 - core, c), device_id_type=MESH)
    own_sib.start()
    to_v = local(act, act_v, local_sem.at[0])
    keep_act = local(act, own_act, local_sem.at[1])

    for i in range(dloc // 128):
        rows = slice(i * 128, (i + 1) * 128)
        gt[rows, :] = go[:, rows].astype(F32).T.astype(BF16)
    half = dloc // 2
    zc, xc = c // 2, c % 2
    pos = (1 - xc) * zc + xc * (ncol - 1 - zc)

    def col_of(p):
        x = p // nz
        return ((1 - x) * p + x * (ncol - 1 - p)) * 2 + x

    def gt_at(col, h):
        if aligned:
            return gt_full.at[pl.ds(h * half, half), pl.ds(pl.multiple_of(col * tok_c, 128), tok_c)]
        return gt_full.at[col, pl.ds(h * half, half), :]

    def ring_halves(k, way):
        return [way, 1 - way] if k < ncol // 2 - 1 else [way]

    def ring_send(k, way, h):
        sign = 1 - 2 * way
        origin = col_of((pos - sign * k + ncol) % ncol)
        target = col_of((pos + sign + ncol) % ncol)
        src = gt.at[pl.ds(h * half, half), :] if k == 0 else gt_at(origin, h)
        send, recv = (cc_s, cc_r) if way else (cw_s, cw_r)
        remote(src, gt_at(origin, h), send.at[k, h], recv.at[k, h], r, target)

    def ring_wait(k, way, h):
        sign = 1 - 2 * way
        origin = col_of((pos - sign * (k + 1) + ncol) % ncol)
        piece = gt_at(origin, h)
        send, recv = (cc_s, cc_r) if way else (cw_s, cw_r)
        pltpu.make_async_remote_copy(
            src_ref=piece, dst_ref=piece, send_sem=send.at[k, h], recv_sem=recv.at[k, h],
            device_id=dev(r, c), device_id_type=MESH).wait_recv()
        if k + 1 < ncol // 2 and h in ring_halves(k + 1, way):
            ring_send(k + 1, way, h)

    for i in range(2):
        for way in range(2):
            ring_send(0, way, ring_halves(0, way)[i])
    if aligned:
        own_gt = gt_full.at[:, pl.ds(pl.multiple_of(c * tok_c, 128), tok_c)]
    else:
        own_gt = gt_full.at[c]
    keep_gt = local(gt, own_gt, local_sem.at[2])

    def first_part():
        lanes_l, lanes_r = l_msg.shape[1] - 128, r_msg.shape[1] - 128
        l_msg[...] = jnp.zeros_like(l_msg)
        l_msg[:, :tok_c] = times_pieces(lpair[...], go[...])
        l_msg[:, lanes_l : lanes_l + HALF] = dot(lpair[...], lpair[HALF:, :], 1, 1)
        to_v.wait()
        r_msg[...] = jnp.zeros_like(r_msg)
        r_msg[:, :tok_r] = times_pieces(rpair[...], act_v[...])
        r_msg[:, lanes_r : lanes_r + HALF] = dot(rpair[...], rpair[HALF:, :], 1, 1)
        l_sum[0] = l_msg[...]
        r_sum[0] = r_msg[...]

    def partner(i, s):
        return i + (1 - 2 * ((i // 2**s) % 2)) * 2**s

    def sum_start(s):
        if s < stages(nrow):
            remote(l_sum.at[s], l_in.at[s], l1_s.at[s], l1_r.at[s], partner(r, s), c)
        if s < stages(ncol):
            remote(r_sum.at[s], r_in.at[s], r1_s.at[s], r1_r.at[s], r, partner(c, s))

    def arrived(ref, send, recv):
        pltpu.make_async_remote_copy(
            src_ref=ref, dst_ref=ref, send_sem=send, recv_sem=recv,
            device_id=dev(r, c), device_id_type=MESH).wait_recv()

    def sum_end(s):
        if s < stages(nrow):
            arrived(l_in.at[s], l1_s.at[s], l1_r.at[s])
            l_sum[s + 1] = l_sum[s] + l_in[s]
        if s < stages(ncol):
            arrived(r_in.at[s], r1_s.at[s], r1_r.at[s])
            r_sum[s + 1] = r_sum[s] + r_in[s]

    ls, rs = stages(nrow), stages(ncol)

    def spread_sums():
        l_own = l_sum.at[ls, :, pl.ds(0, l_all.shape[2])]
        r_own = r_sum.at[rs, :, pl.ds(0, r_all.shape[2])]
        for d in range(1, ncol):
            remote(l_own, l_all.at[c], l2_s.at[d], l2_r.at[d], r, (c + d) % ncol)
        for d in range(1, nrow):
            remote(r_own, r_all.at[r], r2_s.at[d], r2_r.at[d], (r + d) % nrow, c)
        l_all[c] = l_sum[ls, :, : l_all.shape[2]]
        r_all[r] = r_sum[rs, :, : r_all.shape[2]]

    def last_part():
        for d in range(1, ncol):
            arrived(l_all.at[(c + ncol - d) % ncol], l2_s.at[d], l2_r.at[d])
        for d in range(1, nrow):
            arrived(r_all.at[(r + nrow - d) % nrow], r2_s.at[d], r2_r.at[d])
        for i in range(ncol):
            l_cat[:, i * tok_c : (i + 1) * tok_c] = l_all[i, :, :tok_c]
        for i in range(nrow):
            r_cat[:, i * tok_r : (i + 1) * tok_r] = r_all[i, :, :tok_r]
        left = compact(l_sum[ls, :, l_all.shape[2] : l_all.shape[2] + HALF], pairs)
        right = compact(r_sum[rs, :, r_all.shape[2] : r_all.shape[2] + HALF], pairs)
        lf = right[0] * apply_terms(left, l_cat[...])
        rf = left[0] * apply_terms(right, r_cat[...])
        for i, piece in enumerate(pieces(lf, 3)):
            lf_out[i * BOTH : (i + 1) * BOTH, :] = piece.astype(BF16)
        for i, piece in enumerate(pieces(rf, 3)):
            rf_out[i * BOTH : (i + 1) * BOTH, :] = piece.astype(BF16)
        cross = dot(l_cat[...], r_cat[...], 1, 1)
        x2_out[...] = apply_terms(right, dot(cross, apply_terms(left, lpair[...]), 0, 0))
        s_out[...] = jnp.broadcast_to(left[0] * right[0], s_out.shape)

    todo = []
    ring_total = ncol - 1
    for k in range(ncol // 2):
        for i, _ in enumerate(ring_halves(k, 0)):
            for way in range(2):
                h = ring_halves(k, way)[i]
                todo.append(((2 * k + i + 1) / ring_total, functools.partial(ring_wait, k, way, h)))
    y_count = sum(len(y_parts(k, 0)) for k in range(max(ny // 2, 1)))
    done = 0
    for k in range(max(ny // 2, 1)):
        for i in range(len(y_parts(k, 0))):
            done += 1
            for way in range(2):
                todo.append((done / y_count, functools.partial(y_wait, k, way, y_parts(k, way)[i])))
    small = [first_part, functools.partial(sum_start, 0)]
    for s in range(max(ls, rs)):
        small.append((lambda s: lambda: (sum_end(s), sum_start(s + 1)))(s))
    small += [spread_sums, last_part]
    for i, f in enumerate(small):
        todo.append((max(0, i - 1) * spread + 0.001, f))
    todo.sort(key=lambda item: item[0])
    for _, f in todo:
        f()
    own_sib.wait()
    for k in range(max(ny // 2, 1)):
        for way in range(2):
            sign = 1 - 2 * way
            origin = ((y - sign * (k + 1) + 2 * ny) % ny) * 2 + 1 - core
            for part in y_parts(k, way):
                arrived(act_at(origin, part), sib_s.at[way, k, part], sib_r.at[way, k, part])
    keep_act.wait()
    keep_gt.wait()
    for copy in pending:
        copy.wait_send()


def apply_kernel(step_m, s_ref, gt, act, lf, rf, x2, lpair, rpair, out, a_ext, b_ext):
    wide = 2 * BOTH
    dloc = gt.shape[0]

    @pl.when(pl.program_id(0) == 0)
    def _():
        got = bdot(rf[...], gt[...], 1, 1)
        second = got[:BOTH] + got[BOTH : 2 * BOTH] + got[2 * BOTH :] + x2[...]
        hi, lo = pieces(jnp.concatenate([lpair[...], second], 0), 2)
        ext = jnp.concatenate([hi, hi, lo, jnp.zeros_like(hi)], 0)
        for i in range(dloc // 128):
            rows = slice(i * 128, (i + 1) * 128)
            a_ext[rows, :] = ext[:, rows].T.astype(BF16)

    got = bdot(lf[...], act[...], 1, 0)
    first = got[:BOTH] + got[BOTH : 2 * BOTH] + got[2 * BOTH :]
    hi, lo = pieces(jnp.concatenate([first, rpair[...]], 0), 2)
    b_ext[...] = jnp.concatenate([hi, lo, hi, jnp.zeros_like(hi)], 0).astype(BF16)
    scale = s_ref[0:1, 0:1]

    @pl.loop(0, dloc // step_m)
    def _(i):
        rows = pl.ds(pl.multiple_of(i * step_m, step_m), step_m)
        out[rows, :] = scale * bdot(gt[rows, :], act[...], 1, 0) + bdot(a_ext[rows, :], b_ext[...], 1, 0)


def stack_pairs(steps, curves):
    rows = ((0, HALF - steps.shape[0]), (0, 0))
    return jnp.concatenate([jnp.pad(steps, rows), jnp.pad(curves, rows)], 0)


def on_device(nrow, ncol, grad_out, activations, left_steps, left_curves, right_steps, right_curves):
    pairs = left_steps.shape[0]
    tok_c, dloc = grad_out.shape
    tok_r, floc = activations.shape
    tokens = tok_c * ncol
    lpair = stack_pairs(left_steps, left_curves)
    rpair = stack_pairs(right_steps, right_curves)
    aligned = tok_c % 128 == 0
    cuts = max(n for n in (1, 2, 4) if tok_r % (2 * n * 16) == 0)
    wide_c, wide_r = -(-tok_c // 128) * 128, -(-tok_r // 128) * 128
    ls, rs = stages(nrow), stages(ncol)
    hops_y = max(nrow // 4, 1)
    dma = pltpu.SemaphoreType.DMA
    vmem, anyw = pl.BlockSpec(memory_space=pltpu.VMEM), pl.BlockSpec(memory_space=pl.ANY)
    gt_shape = (dloc, tokens) if aligned else (ncol, dloc, tok_c)
    act_full, gt, lf, rf, x2, s = pl.pallas_call(
        functools.partial(gather_kernel, nrow, ncol, pairs, aligned, cuts, 0.12),
        out_shape=[
            jax.ShapeDtypeStruct((tokens, floc), BF16),
            jax.ShapeDtypeStruct(gt_shape, BF16),
            jax.ShapeDtypeStruct((3 * BOTH, tokens), BF16),
            jax.ShapeDtypeStruct((3 * BOTH, tokens), BF16),
            jax.ShapeDtypeStruct((BOTH, dloc), F32),
            jax.ShapeDtypeStruct((8, 128), F32),
        ],
        in_specs=[anyw, vmem, vmem, vmem],
        out_specs=[anyw, anyw, vmem, vmem, vmem, vmem],
        scratch_shapes=[
            pltpu.VMEM((dloc, tok_c), BF16),
            pltpu.VMEM((tok_r, floc), BF16),
            pltpu.VMEM((BOTH, wide_c + 128), F32),
            pltpu.VMEM((BOTH, wide_r + 128), F32),
            pltpu.VMEM((ls, BOTH, wide_c + 128), F32),
            pltpu.VMEM((rs, BOTH, wide_r + 128), F32),
            pltpu.VMEM((ls + 1, BOTH, wide_c + 128), F32),
            pltpu.VMEM((rs + 1, BOTH, wide_r + 128), F32),
            pltpu.VMEM((ncol, BOTH, wide_c), F32),
            pltpu.VMEM((nrow, BOTH, wide_r), F32),
            pltpu.VMEM((BOTH, tokens), F32),
            pltpu.VMEM((BOTH, tokens), F32),
            dma((5,)),
            dma((ncol // 2, 2)), dma((ncol // 2, 2)), dma((ncol // 2, 2)), dma((ncol // 2, 2)),
            dma((2, hops_y, 2 * cuts)), dma((2, hops_y, 2 * cuts)),
            dma((2, hops_y, 2 * cuts)), dma((2, hops_y, 2 * cuts)),
            dma((ls,)), dma((ls,)), dma((rs,)), dma((rs,)),
            dma((ncol,)), dma((ncol,)), dma((nrow,)), dma((nrow,)),
        ],
        compiler_params=pltpu.CompilerParams(
            collective_id=0, has_side_effects=True, vmem_limit_bytes=40 * 2**20),
        name="gather",
    )(activations, grad_out, lpair, rpair)
    if not aligned:
        gt = jnp.transpose(gt, (1, 0, 2)).reshape(dloc, tokens)
    step_n = max(n for n in (128, 256, 512) if floc % n == 0)
    step_m = min(512, dloc)

    def whole(shape):
        return pl.BlockSpec(shape, lambda j: (0, 0), pipeline_mode=pl.Buffered(1))

    return pl.pallas_call(
        functools.partial(apply_kernel, step_m),
        grid=(floc // step_n,),
        out_shape=jax.ShapeDtypeStruct((dloc, floc), F32),
        in_specs=[
            whole((8, 128)),
            whole((dloc, tokens)),
            pl.BlockSpec((tokens, step_n), lambda j: (0, j)),
            whole((3 * BOTH, tokens)),
            whole((3 * BOTH, tokens)),
            whole((BOTH, dloc)),
            whole((BOTH, dloc)),
            pl.BlockSpec((BOTH, step_n), lambda j: (0, j)),
        ],
        out_specs=pl.BlockSpec((dloc, step_n), lambda j: (0, j)),
        scratch_shapes=[pltpu.VMEM((dloc, 8 * BOTH), BF16), pltpu.VMEM((8 * BOTH, step_n), BF16)],
        compiler_params=pltpu.CompilerParams(vmem_limit_bytes=48 * 2**20),
        cost_estimate=pl.CostEstimate(
            flops=2 * dloc * floc * tokens, bytes_accessed=4 * dloc * floc, transcendentals=0),
        name="apply",
    )(s, gt, act_full, lf, rf, x2, lpair, rpair)


def solution(mesh):
    in_specs = (
        P("col", "row"),
        P("row", "col"),
        P(None, "row"),
        P(None, "row"),
        P(None, "col"),
        P(None, "col"),
    )
    out_specs = P("row", "col")
    body = functools.partial(on_device, mesh.shape["row"], mesh.shape["col"])
    return jax.shard_map(body, mesh=mesh, in_specs=in_specs, out_specs=out_specs, check_vma=False)
```

time: 445 us -> 201 us (0.45); the launches traced: 438 us -> 200 us
  matrix products: 215 us -> 0 us
  Pallas kernels: 0 us -> 194 us
  blocking collectives: 83 us -> 0 us
  other arithmetic: 68.8 us -> 2.07 us
  waiting for transfers between devices: 46.9 us -> 0 us
  between operations: 16.2 us -> 0.02 us
  local copies, waits for them, and re-layouts: 8.38 us -> 3.26 us
    dot_general x23 -> x0, matrix products: 215 us -> none  [the longest x1 63.5 us: on_device(): lax.dot_general(shard_piece, token_panel, contract, preferred_element_typ...]
    pallas_call x0 -> x2, Pallas kernels: none -> 194 us  [the longest x1 143 us: on_device(): pl.pallas_call(functools.partial(gather_kernel, nrow, ncol, pairs, aligne...]
    div x2 -> x0, other arithmetic: 68.6 us -> none  [upper_inverse(): inv_rows[index] = running / upper_tri[index, index]]
    psum x2 -> x0, blocking collectives: 52 us -> none  [the longest x1 38.7 us: on_device(): lax.psum((right_sy, right_yy, right_part), 'col')]
    psum x1 -> x0, waiting for transfers between devices: 39.8 us -> none  [on_device(): lax.psum((right_sy, right_yy, right_part), 'col')]
    all_gather x1 -> x0, blocking collectives: 31 us -> none  [on_device(): left_full = lax.all_gather(left_part, 'col', axis=0, tiled=True)]
    slice x10 -> x0, local copies, waits for them, and re-layouts: 6.86 us -> none  [the longest x4 2.88 us: upper_inverse(): inv_rows[index] = running / upper_tri[index, index]]
    all_gather x2 -> x0, waiting for transfers between devices: 5.67 us -> none  [the longest x1 5.65 us: on_device(): token_panel = lax.all_gather(activations, 'row', axis=0, tiled=True)]
  transfers between devices with their start and end apart: 3 -> 0, of which waited for: 2 -> 0; matrix products, arithmetic and copies ran while one was open for 38% -> 0% of each run, Pallas kernels for 0% -> 0%
where the time goes in v1:
time: 201 us; the launch traced here: 200 us
  Pallas kernels  194 us (97%)
  local copies, waits for them, and re-layouts  3.26 us (2%)
  other arithmetic  2.07 us (1%)
    pallas_call x1, Pallas kernels, on_device(): pl.pallas_call(functools.partial(gather_kernel, nrow, ncol, pairs, aligne...  143 us
    pallas_call x1, Pallas kernels, on_device(): pl.pallas_call(functools.partial(apply_kernel, step_m), grid=(floc // ste...  51.3 us

profile of v1, /device:TPU:0, one launch (start us, length us, event | category | flops | bytes accessed | tf_op | source)
XLA Modules:
  0.0 199.6 jit_solution(13340011312725189166)
XLA Ops:
  0.0 1.0 select_maximum_fusion.1.lpair
  1.0 1.1 select_maximum_fusion.rpair
  2.1 0.0 copy-start
  2.1 2.0 %copy-done = bf16[512,3584]{1,0:T(8,128)(2,1)S(1)} copy-done((bf16[512,3584]{1,0:T(8,128)(2,1)S(1)}, bf16[512,3584]{1,0:T(8,128)(2,1)}, u32[]{:S(2)}) %copy-start) | copy-done | bytes 3670040
  4.1 0.0 copy-start.1
  4.1 1.2 copy-done.1
  5.3 142.9 %gather.1 = (bf16[2048,3584]{1,0:T(8,128)(2,1)}, bf16[2048,2048]{1,0:T(8,128)(2,1)}, bf16[96,2048]{1,0:T(8,128)(2,1)S(1)}, bf16[96,2048]{1,0:T(8,128)(2,1)S(1)},...) custom-call(bf16[512,3584]{1,0:T(8,128)(2,1)S(1)} %copy-done, bf16[256,2048]{1,0:T(8,128)(2,1)S(1)} %copy-done.1, ...), custom_call_target="tpu_custom_call" | custom-call | tf_op jit(solution)/shard_map/gather/pallas_call | solution.py:355
  148.3 51.3 %apply.1 = f32[2048,3584]{1,0:T(8,128)} custom-call(f32[8,128]{1,0:T(8,128)S(1)} %get-tuple-element.11.s_ref, bf16[2048,2048]{1,0:T(8,128)(2,1)} %get-tuple-element.12.gt, bf16[2048,3584]{1,0:T(8,128)(2,1)} %get-tuple-element.13.act, bf16[96,2048]{1,0:T(8,128)(2,1)S(1)} %get-tuple-element.14.lf, bf16[96,2048]{1,0:T(8,128)(2,1)S(1)} %get-tuple-element.15.rf, ...), custom_call_target="tpu_custom_call" | custom-call | flops 30064771072 | bytes 29360128 | tf_op jit(solution)/shard_map/apply/pallas_call | solution.py:399
Async XLA Ops:
  2.1 2.0 %copy-start = (bf16[512,3584]{1,0:T(8,128)(2,1)S(1)}, bf16[512,3584]{1,0:T(8,128)(2,1)}, u32[]{:S(2)}) copy-start(bf16[512,3584]{1,0:T(8,128)(2,1)} %act.1) | copy-start | bytes 11010052
  4.1 1.2 copy-start.1

commit v2 on v1

--- a/solution.py
+++ b/solution.py
@@ -71,11 +71,11 @@
 
 
 def gather_kernel(
-    nrow, ncol, pairs, aligned, cuts, spread,
+    nrow, ncol, pairs, aligned, cuts, fine, spread,
     act, go, lpair, rpair,
     act_full, gt_full, lf_out, rf_out, x2_out, s_out,
     gt, act_v, l_msg, r_msg, l_in, r_in, l_sum, r_sum, l_all, r_all, l_cat, r_cat,
-    local_sem, cw_s, cw_r, cc_s, cc_r, y_s, y_r, sib_s, sib_r,
+    local_sem, own_s, own_r, cw_s, cw_r, cc_s, cc_r, y_s, y_r, sib_s, sib_r,
     l1_s, l1_r, r1_s, r1_r, l2_s, l2_r, r2_s, r2_r,
 ):
     r, c = lax.axis_index("row"), lax.axis_index("col")
@@ -141,25 +141,21 @@
         if k + 1 < max(ny // 2, 1) and part in y_parts(k + 1, way):
             y_send(k + 1, way, part)
 
-    for part in range(cuts):
-        y_send(0, 0, part)
-        y_send(0, 1, cuts + part)
-    if ny > 2:
-        for part in range(cuts):
-            y_send(0, 0, cuts + part)
-            y_send(0, 1, part)
+    def y_first(i):
+        for way in range(2):
+            y_send(0, way, y_parts(0, way)[i])
+
     own_act = act_full.at[pl.ds(pl.multiple_of(r * tok_r, 16), tok_r), :]
-    own_sib = pltpu.make_async_remote_copy(
-        src_ref=act, dst_ref=own_act, send_sem=local_sem.at[3], recv_sem=local_sem.at[4],
-        device_id=dev(y * 2 + 1 - core, c), device_id_type=MESH)
-    own_sib.start()
     to_v = local(act, act_v, local_sem.at[0])
-    keep_act = local(act, own_act, local_sem.at[1])
+
+    def own_sibling(part):
+        src = act.at[pl.ds(part * step_a, step_a), :]
+        remote(src, act_at(r, part), own_s.at[part], own_r.at[part], y * 2 + 1 - core, c)
 
     for i in range(dloc // 128):
         rows = slice(i * 128, (i + 1) * 128)
         gt[rows, :] = go[:, rows].astype(F32).T.astype(BF16)
-    half = dloc // 2
+    half = dloc // (2 * fine)
     zc, xc = c // 2, c % 2
     pos = (1 - xc) * zc + xc * (ncol - 1 - zc)
 
@@ -173,7 +169,10 @@
         return gt_full.at[col, pl.ds(h * half, half), :]
 
     def ring_halves(k, way):
-        return [way, 1 - way] if k < ncol // 2 - 1 else [way]
+        groups = [list(range(way * fine, (way + 1) * fine))]
+        if k < ncol // 2 - 1:
+            groups.append(list(range((1 - way) * fine, (2 - way) * fine)))
+        return sum(groups, [])
 
     def ring_send(k, way, h):
         sign = 1 - 2 * way
@@ -194,9 +193,11 @@
         if k + 1 < ncol // 2 and h in ring_halves(k + 1, way):
             ring_send(k + 1, way, h)
 
-    for i in range(2):
+    for i in range(2 * fine):
         for way in range(2):
             ring_send(0, way, ring_halves(0, way)[i])
+        if i < 2:
+            y_first(i)
     if aligned:
         own_gt = gt_full.at[:, pl.ds(pl.multiple_of(c * tok_c, 128), tok_c)]
     else:
@@ -271,29 +272,40 @@
         s_out[...] = jnp.broadcast_to(left[0] * right[0], s_out.shape)
 
     todo = []
-    ring_total = ncol - 1
+    ring_total = (ncol - 1) * fine
+    done = 0
     for k in range(ncol // 2):
-        for i, _ in enumerate(ring_halves(k, 0)):
+        for i in range(len(ring_halves(k, 0))):
+            done += 1
             for way in range(2):
                 h = ring_halves(k, way)[i]
-                todo.append(((2 * k + i + 1) / ring_total, functools.partial(ring_wait, k, way, h)))
+                todo.append((done / ring_total, functools.partial(ring_wait, k, way, h)))
     y_count = sum(len(y_parts(k, 0)) for k in range(max(ny // 2, 1)))
     done = 0
     for k in range(max(ny // 2, 1)):
         for i in range(len(y_parts(k, 0))):
+            if k == 0 and i >= 2:
+                todo.append(((i - 1.5) / y_count, functools.partial(y_first, i)))
             done += 1
             for way in range(2):
-                todo.append((done / y_count, functools.partial(y_wait, k, way, y_parts(k, way)[i])))
+                todo.append((done / y_count + 0.2, functools.partial(y_wait, k, way, y_parts(k, way)[i])))
+    for part in range(2 * cuts):
+        todo.append((0.1 + 0.8 * part / (2 * cuts), functools.partial(own_sibling, part)))
+    keep_act = pltpu.make_async_copy(act, own_act, local_sem.at[1])
+    todo.append((0.35, keep_act.start))
     small = [first_part, functools.partial(sum_start, 0)]
     for s in range(max(ls, rs)):
         small.append((lambda s: lambda: (sum_end(s), sum_start(s + 1)))(s))
     small += [spread_sums, last_part]
-    for i, f in enumerate(small):
+    for i, f in enumerate(small[:-2]):
         todo.append((max(0, i - 1) * spread + 0.001, f))
+    late = max(ls, rs) * spread + 0.002
+    todo += [(late, small[-2]), (late + 1.5 * spread, small[-1])]
     todo.sort(key=lambda item: item[0])
     for _, f in todo:
         f()
-    own_sib.wait()
+    for part in range(2 * cuts):
+        arrived(act_at(y * 2 + 1 - core, part), own_s.at[part], own_r.at[part])
     for k in range(max(ny // 2, 1)):
         for way in range(2):
             sign = 1 - 2 * way
@@ -345,7 +357,8 @@
     lpair = stack_pairs(left_steps, left_curves)
     rpair = stack_pairs(right_steps, right_curves)
     aligned = tok_c % 128 == 0
-    cuts = max(n for n in (1, 2, 4) if tok_r % (2 * n * 16) == 0)
+    cuts = max(n for n in (1, 2, 4, 8) if tok_r % (2 * n * 16) == 0)
+    fine = max(n for n in (1, 2) if dloc % (2 * n * 16) == 0)
     wide_c, wide_r = -(-tok_c // 128) * 128, -(-tok_r // 128) * 128
     ls, rs = stages(nrow), stages(ncol)
     hops_y = max(nrow // 4, 1)
@@ -353,7 +366,7 @@
     vmem, anyw = pl.BlockSpec(memory_space=pltpu.VMEM), pl.BlockSpec(memory_space=pl.ANY)
     gt_shape = (dloc, tokens) if aligned else (ncol, dloc, tok_c)
     act_full, gt, lf, rf, x2, s = pl.pallas_call(
-        functools.partial(gather_kernel, nrow, ncol, pairs, aligned, cuts, 0.12),
+        functools.partial(gather_kernel, nrow, ncol, pairs, aligned, cuts, fine, 0.15),
         out_shape=[
             jax.ShapeDtypeStruct((tokens, floc), BF16),
             jax.ShapeDtypeStruct(gt_shape, BF16),
@@ -377,8 +390,9 @@
             pltpu.VMEM((nrow, BOTH, wide_r), F32),
             pltpu.VMEM((BOTH, tokens), F32),
             pltpu.VMEM((BOTH, tokens), F32),
-            dma((5,)),
-            dma((ncol // 2, 2)), dma((ncol // 2, 2)), dma((ncol // 2, 2)), dma((ncol // 2, 2)),
+            dma((3,)),
+            dma((2 * cuts,)), dma((2 * cuts,)),
+            dma((ncol // 2, 2 * fine)), dma((ncol // 2, 2 * fine)), dma((ncol // 2, 2 * fine)), dma((ncol // 2, 2 * fine)),
             dma((2, hops_y, 2 * cuts)), dma((2, hops_y, 2 * cuts)),
             dma((2, hops_y, 2 * cuts)), dma((2, hops_y, 2 * cuts)),
             dma((ls,)), dma((ls,)), dma((rs,)), dma((rs,)),

time: 201 us -> 156 us (0.78)
  Pallas kernels: 194 us -> 150 us
    pallas_call x1, Pallas kernels: 143 us -> 98.8 us  [on_device(): pl.pallas_call(functools.partial(gather_kernel, nrow, ncol, pairs, aligne...]
where the time goes in v2:
time: 156 us; the launch traced here: 155 us
  Pallas kernels  150 us (96%)
  local copies, waits for them, and re-layouts  3.26 us (2%)
  other arithmetic  2.07 us (1%)
    pallas_call x1, Pallas kernels, on_device(): pl.pallas_call(functools.partial(gather_kernel, nrow, ncol, pairs, aligne...  98.8 us
    pallas_call x1, Pallas kernels, on_device(): pl.pallas_call(functools.partial(apply_kernel, step_m), grid=(floc // ste...  51.3 us
    unnamed x4, local copies, waits for them, and re-layouts  3.26 us

profile of v2, /device:TPU:0, one launch (start us, length us, event | category | flops | bytes accessed | tf_op | source)
XLA Modules:
  0.0 155.5 jit_solution(15012517593270428458)
XLA Ops:
  0.0 1.0 select_maximum_fusion.1.lpair
  1.0 1.1 select_maximum_fusion.rpair
  2.1 0.0 copy-start
  2.1 2.0 %copy-done = bf16[512,3584]{1,0:T(8,128)(2,1)S(1)} copy-done((bf16[512,3584]{1,0:T(8,128)(2,1)S(1)}, bf16[512,3584]{1,0:T(8,128)(2,1)}, u32[]{:S(2)}) %copy-start) | copy-done | bytes 3670040
  4.1 0.0 copy-start.1
  4.1 1.2 copy-done.1
  5.3 98.8 %gather.1 = (bf16[2048,3584]{1,0:T(8,128)(2,1)}, bf16[2048,2048]{1,0:T(8,128)(2,1)}, bf16[96,2048]{1,0:T(8,128)(2,1)S(1)}, bf16[96,2048]{1,0:T(8,128)(2,1)S(1)},...) custom-call(bf16[512,3584]{1,0:T(8,128)(2,1)S(1)} %copy-done, bf16[256,2048]{1,0:T(8,128)(2,1)S(1)} %copy-done.1, ...), custom_call_target="tpu_custom_call" | custom-call | tf_op jit(solution)/shard_map/gather/pallas_call | solution.py:368
  104.1 51.3 %apply.1 = f32[2048,3584]{1,0:T(8,128)} custom-call(f32[8,128]{1,0:T(8,128)S(1)} %get-tuple-element.11.s_ref, bf16[2048,2048]{1,0:T(8,128)(2,1)} %get-tuple-element.12.gt, bf16[2048,3584]{1,0:T(8,128)(2,1)} %get-tuple-element.13.act, bf16[96,2048]{1,0:T(8,128)(2,1)S(1)} %get-tuple-element.14.lf, bf16[96,2048]{1,0:T(8,128)(2,1)S(1)} %get-tuple-element.15.rf, ...), custom_call_target="tpu_custom_call" | custom-call | flops 30064771072 | bytes 29360128 | tf_op jit(solution)/shard_map/apply/pallas_call | solution.py:413
Async XLA Ops:
  2.1 2.0 %copy-start = (bf16[512,3584]{1,0:T(8,128)(2,1)S(1)}, bf16[512,3584]{1,0:T(8,128)(2,1)}, u32[]{:S(2)}) copy-start(bf16[512,3584]{1,0:T(8,128)(2,1)} %act.1) | copy-start | bytes 11010052
  4.1 1.2 copy-start.1

commit v3 on v2

--- a/solution.py
+++ b/solution.py
@@ -72,10 +72,10 @@
 
 def gather_kernel(
     nrow, ncol, pairs, aligned, cuts, fine, spread,
-    act, go, lpair, rpair,
+    act, go_any, lpair, rpair,
     act_full, gt_full, lf_out, rf_out, x2_out, s_out,
-    gt, act_v, l_msg, r_msg, l_in, r_in, l_sum, r_sum, l_all, r_all, l_cat, r_cat,
-    local_sem, own_s, own_r, cw_s, cw_r, cc_s, cc_r, y_s, y_r, sib_s, sib_r,
+    go, gt, act_v, l_msg, r_msg, l_in, r_in, l_sum, r_sum, l_all, r_all, l_cat, r_cat,
+    go_sem, local_sem, own_s, own_r, cw_s, cw_r, cc_s, cc_r, y_s, y_r, sib_s, sib_r,
     l1_s, l1_r, r1_s, r1_r, l2_s, l2_r, r2_s, r2_r,
 ):
     r, c = lax.axis_index("row"), lax.axis_index("col")
@@ -87,6 +87,8 @@
     def dev(row, col):
         return {"row": row, "col": col}
 
+    to_go = pltpu.make_async_copy(go_any, go, go_sem)
+    to_go.start()
     barrier = pltpu.get_barrier_semaphore()
     for d in range(1, nrow):
         pl.semaphore_signal(barrier, inc=1, device_id=dev((r + d) % nrow, c), device_id_type=MESH)
@@ -152,6 +154,7 @@
         src = act.at[pl.ds(part * step_a, step_a), :]
         remote(src, act_at(r, part), own_s.at[part], own_r.at[part], y * 2 + 1 - core, c)
 
+    to_go.wait()
     for i in range(dloc // 128):
         rows = slice(i * 128, (i + 1) * 128)
         gt[rows, :] = go[:, rows].astype(F32).T.astype(BF16)
@@ -263,9 +266,9 @@
         right = compact(r_sum[rs, :, r_all.shape[2] : r_all.shape[2] + HALF], pairs)
         lf = right[0] * apply_terms(left, l_cat[...])
         rf = left[0] * apply_terms(right, r_cat[...])
-        for i, piece in enumerate(pieces(lf, 3)):
+        for i, piece in enumerate(pieces(lf, 2)):
             lf_out[i * BOTH : (i + 1) * BOTH, :] = piece.astype(BF16)
-        for i, piece in enumerate(pieces(rf, 3)):
+        for i, piece in enumerate(pieces(rf, 2)):
             rf_out[i * BOTH : (i + 1) * BOTH, :] = piece.astype(BF16)
         cross = dot(l_cat[...], r_cat[...], 1, 1)
         x2_out[...] = apply_terms(right, dot(cross, apply_terms(left, lpair[...]), 0, 0))
@@ -325,7 +328,7 @@
     @pl.when(pl.program_id(0) == 0)
     def _():
         got = bdot(rf[...], gt[...], 1, 1)
-        second = got[:BOTH] + got[BOTH : 2 * BOTH] + got[2 * BOTH :] + x2[...]
+        second = got[:BOTH] + got[BOTH:] + x2[...]
         hi, lo = pieces(jnp.concatenate([lpair[...], second], 0), 2)
         ext = jnp.concatenate([hi, hi, lo, jnp.zeros_like(hi)], 0)
         for i in range(dloc // 128):
@@ -333,7 +336,7 @@
             a_ext[rows, :] = ext[:, rows].T.astype(BF16)
 
     got = bdot(lf[...], act[...], 1, 0)
-    first = got[:BOTH] + got[BOTH : 2 * BOTH] + got[2 * BOTH :]
+    first = got[:BOTH] + got[BOTH:]
     hi, lo = pieces(jnp.concatenate([first, rpair[...]], 0), 2)
     b_ext[...] = jnp.concatenate([hi, lo, hi, jnp.zeros_like(hi)], 0).astype(BF16)
     scale = s_ref[0:1, 0:1]
@@ -370,14 +373,15 @@
         out_shape=[
             jax.ShapeDtypeStruct((tokens, floc), BF16),
             jax.ShapeDtypeStruct(gt_shape, BF16),
-            jax.ShapeDtypeStruct((3 * BOTH, tokens), BF16),
-            jax.ShapeDtypeStruct((3 * BOTH, tokens), BF16),
+            jax.ShapeDtypeStruct((2 * BOTH, tokens), BF16),
+            jax.ShapeDtypeStruct((2 * BOTH, tokens), BF16),
             jax.ShapeDtypeStruct((BOTH, dloc), F32),
             jax.ShapeDtypeStruct((8, 128), F32),
         ],
-        in_specs=[anyw, vmem, vmem, vmem],
+        in_specs=[anyw, anyw, vmem, vmem],
         out_specs=[anyw, anyw, vmem, vmem, vmem, vmem],
         scratch_shapes=[
+            pltpu.VMEM((tok_c, dloc), BF16),
             pltpu.VMEM((dloc, tok_c), BF16),
             pltpu.VMEM((tok_r, floc), BF16),
             pltpu.VMEM((BOTH, wide_c + 128), F32),
@@ -390,7 +394,7 @@
             pltpu.VMEM((nrow, BOTH, wide_r), F32),
             pltpu.VMEM((BOTH, tokens), F32),
             pltpu.VMEM((BOTH, tokens), F32),
-            dma((3,)),
+            dma(()), dma((3,)),
             dma((2 * cuts,)), dma((2 * cuts,)),
             dma((ncol // 2, 2 * fine)), dma((ncol // 2, 2 * fine)), dma((ncol // 2, 2 * fine)), dma((ncol // 2, 2 * fine)),
             dma((2, hops_y, 2 * cuts)), dma((2, hops_y, 2 * cuts)),
@@ -405,7 +409,7 @@
     if not aligned:
         gt = jnp.transpose(gt, (1, 0, 2)).reshape(dloc, tokens)
     step_n = max(n for n in (128, 256, 512) if floc % n == 0)
-    step_m = min(512, dloc)
+    step_m = min(1024, dloc)
 
     def whole(shape):
         return pl.BlockSpec(shape, lambda j: (0, 0), pipeline_mode=pl.Buffered(1))
@@ -418,8 +422,8 @@
             whole((8, 128)),
             whole((dloc, tokens)),
             pl.BlockSpec((tokens, step_n), lambda j: (0, j)),
-            whole((3 * BOTH, tokens)),
-            whole((3 * BOTH, tokens)),
+            whole((2 * BOTH, tokens)),
+            whole((2 * BOTH, tokens)),
             whole((BOTH, dloc)),
             whole((BOTH, dloc)),
             pl.BlockSpec((BOTH, step_n), lambda j: (0, j)),

time: 156 us -> 153 us (0.981)
  Pallas kernels: 150 us -> 148 us
    pallas_call x1, Pallas kernels: 51.3 us -> 48.9 us  [on_device(): pl.pallas_call(functools.partial(apply_kernel, step_m), grid=(floc // ste...]
where the time goes in v3:
time: 153 us
  Pallas kernels  148 us (97%)
  local copies, waits for them, and re-layouts  3.26 us (2%)
  other arithmetic  2.07 us (1%)
    pallas_call x1, Pallas kernels, on_device(): pl.pallas_call(functools.partial(gather_kernel, nrow, ncol, pairs, aligne...  98.9 us
    pallas_call x1, Pallas kernels, on_device(): pl.pallas_call(functools.partial(apply_kernel, step_m), grid=(floc // ste...  48.9 us
    unnamed x4, local copies, waits for them, and re-layouts  3.26 us

profile of v3, /device:TPU:0, one launch (start us, length us, event | category | flops | bytes accessed | tf_op | source)
XLA Modules:
  0.0 153.1 jit_solution(11665694183340891851)
XLA Ops:
  0.0 1.0 select_maximum_fusion.1.lpair
  1.0 1.1 select_maximum_fusion.rpair
  2.1 0.0 copy-start
  2.1 2.0 %copy-done = bf16[512,3584]{1,0:T(8,128)(2,1)S(1)} copy-done((bf16[512,3584]{1,0:T(8,128)(2,1)S(1)}, bf16[512,3584]{1,0:T(8,128)(2,1)}, u32[]{:S(2)}) %copy-start) | copy-done | bytes 3670040
  4.1 0.0 copy-start.1
  4.1 1.2 copy-done.1
  5.3 98.9 %gather.1 = (bf16[2048,3584]{1,0:T(8,128)(2,1)}, bf16[2048,2048]{1,0:T(8,128)(2,1)}, bf16[64,2048]{1,0:T(8,128)(2,1)S(1)}, bf16[64,2048]{1,0:T(8,128)(2,1)S(1)},...) custom-call(bf16[512,3584]{1,0:T(8,128)(2,1)S(1)} %copy-done, bf16[256,2048]{1,0:T(8,128)(2,1)S(1)} %copy-done.1, ...), custom_call_target="tpu_custom_call" | custom-call | tf_op jit(solution)/shard_map/gather/pallas_call | solution.py:371
  104.3 48.9 %apply.1 = f32[2048,3584]{1,0:T(8,128)} custom-call(f32[8,128]{1,0:T(8,128)S(1)} %get-tuple-element.11.s_ref, bf16[2048,2048]{1,0:T(8,128)(2,1)} %get-tuple-element.12.gt, bf16[2048,3584]{1,0:T(8,128)(2,1)} %get-tuple-element.13.act, bf16[64,2048]{1,0:T(8,128)(2,1)S(1)} %get-tuple-element.14.lf, bf16[64,2048]{1,0:T(8,128)(2,1)S(1)} %get-tuple-element.15.rf, ...), custom_call_target="tpu_custom_call" | custom-call | flops 30064771072 | bytes 29360128 | tf_op jit(solution)/shard_map/apply/pallas_call | solution.py:417
Async XLA Ops:
  2.1 2.0 %copy-start = (bf16[512,3584]{1,0:T(8,128)(2,1)S(1)}, bf16[512,3584]{1,0:T(8,128)(2,1)}, u32[]{:S(2)}) copy-start(bf16[512,3584]{1,0:T(8,128)(2,1)} %act.1) | copy-start | bytes 11010052
  4.1 1.2 copy-start.1
